TPU v7x, 32 devices: a whole 2x2x4 slice. The times are simulated.
32 devices in a mesh: wide: 8 (over y, x, core), narrow: 4 (over z).
Axes of the slice: x: 2, y: 2, z: 4, core: 2. Of those that a mesh axis runs over, the one named last changes fastest.
Arguments:
- state: float32 [2, 8388608], P(None, ('wide', 'narrow')), may hold values from -6 to 6
- gates: float32 [8, 2, 64, 64], replicated, may hold values from -0.5 to 0.5
- roster: int32 [10], replicated, may hold values from 0 to 7
Outputs:
- final_state: float32 [2, 8388608], P(None, ('wide', 'narrow'))
All inputs are finite; a program needn't handle non-finite values.
Results may differ from a plain program's by a relative error of at most 0.00012.
Values sent between devices are 32-bit elements; how exact they have to be, the bound alone decides.
A program may use at most 64 MiB of HBM per device.

v0:
```python
import functools

import jax
import jax.numpy as jnp
from jax import lax
from jax.experimental import pallas as pl
from jax.experimental.pallas import tpu as pltpu
from jax.sharding import PartitionSpec as P

ROUNDS = 2
GATE = 64
LANES = 128
PER_CHUNK = 4
MESH = pl.DeviceIdType.MESH


def block_of(gate):
    re, im = gate[0], gate[1]
    top = jnp.concatenate([re, -im], axis=1)
    bottom = jnp.concatenate([im, re], axis=1)
    return jnp.concatenate([top, bottom], axis=0)


def halves(value):
    high = value.astype(jnp.bfloat16)
    return high, (value - high.astype(jnp.float32)).astype(jnp.bfloat16)


def left_of(block):
    high, low = halves(block)
    top = jnp.concatenate([high, high], axis=1)
    bottom = jnp.concatenate([low, jnp.zeros_like(low)], axis=1)
    return jnp.concatenate([top, bottom], axis=0)


def apply(left, amps):
    high, low = halves(amps)
    out = jnp.dot(
        left, jnp.concatenate([high, low], axis=0), preferred_element_type=jnp.float32
    )
    return out[: 2 * GATE] + out[2 * GATE :]


def weave(first, second):
    low = lax.broadcasted_iota(jnp.int32, first.shape, 1) < LANES // 2
    turned_first = pltpu.roll(first, LANES // 2, 1)
    turned_second = pltpu.roll(second, LANES // 2, 1)
    return jnp.where(low, first, turned_second), jnp.where(low, turned_first, second)


def rows_of(parts):
    return jnp.concatenate(parts, axis=0)


def kernel(narrow, wide, gates_hbm, roster_hbm, x_hbm, out_ref, gates_ref, roster_ref, x_ref,
           left_ref, plane, mixed, send_n, recv_n, send_w, recv_w, load_sem,
           sent_n, came_n, sent_w, came_w):
    me_n, me_w = lax.axis_index("narrow"), lax.axis_index("wide")
    blocks = x_ref.shape[0] // (2 * GATE)
    half = blocks // 2
    chunks = half // PER_CHUNK
    rows_n, rows_w = GATE // narrow, GATE // wide
    split_rows = blocks * GATE
    block_rows = 2 * GATE

    loads = [
        pltpu.make_async_copy(roster_hbm, roster_ref, load_sem.at[0]),
        pltpu.make_async_copy(gates_hbm, gates_ref, load_sem.at[1]),
        pltpu.make_async_copy(x_hbm, x_ref, load_sem.at[2]),
    ]
    for load in loads:
        load.start()

    barrier = pltpu.get_barrier_semaphore()

    def greet_n(d, _):
        pl.semaphore_signal(barrier, inc=1, device_id={"narrow": lax.rem(me_n + d, narrow)}, device_id_type=MESH)
        return 0

    def greet_w(d, _):
        pl.semaphore_signal(barrier, inc=1, device_id={"wide": lax.rem(me_w + d, wide)}, device_id_type=MESH)
        return 0

    lax.fori_loop(1, narrow, greet_n, 0)
    lax.fori_loop(1, wide, greet_w, 0)

    def bank(k):
        return block_of(gates_ref[roster_ref[k]])

    loads[0].wait()
    loads[1].wait()
    for i in range(2):
        left_ref[i] = left_of(bank(i))

    def keep(split, ap, y):
        for c in range(2):
            start = pl.multiple_of(split * split_rows + c * half * GATE + ap * GATE, GATE)
            plane[pl.ds(start, GATE), :] = y[c * GATE:(c + 1) * GATE]

    def first(split):
        def step(i, _):
            parts = []
            for q in range(2):
                pair = [
                    rows_of([x_ref[pl.ds(a * block_rows + c, GATE, stride=2), :] for c in range(2)])
                    for a in (2 * i + q, 2 * i + q + half)
                ]
                parts.append(weave(*pair)[split])
            y = apply(left_ref[0], jnp.concatenate(parts, axis=1))
            for q in range(2):
                keep(split, 2 * i + q, y[:, q * LANES:(q + 1) * LANES])
            return 0

        lax.fori_loop(0, half // 2, step, 0)

    def second(phase, ch):
        rnd, split = phase // 2, phase % 2
        for p in range(PER_CHUNK // 2):
            parts = []
            for q in range(2):
                unit = ch * PER_CHUNK + 2 * p + q
                rows = []
                for c in range(2):
                    base = split * split_rows + c * half * GATE + unit
                    rows += weave(
                        plane[pl.ds(base, blocks, stride=blocks), :],
                        plane[pl.ds(base + half, blocks, stride=blocks), :],
                    )
                parts.append(rows_of(rows))
            y = apply(left_ref[4 * rnd + 1], jnp.concatenate(parts, axis=1))
            for q in range(2):
                for c in range(2):
                    for n in range(narrow):
                        at = ((2 * p + q) * 2 + c) * rows_n
                        send_n[phase, ch, n, at:at + rows_n, :] = y[
                            c * GATE + n * rows_n:c * GATE + (n + 1) * rows_n,
                            q * LANES:(q + 1) * LANES,
                        ]
        for d in range(1, narrow):
            to = lax.rem(me_n + d, narrow)
            pltpu.make_async_remote_copy(
                src_ref=send_n.at[phase, ch, to],
                dst_ref=recv_n.at[phase, ch, me_n],
                send_sem=sent_n.at[phase, ch],
                recv_sem=came_n.at[phase, ch],
                device_id={"narrow": to},
                device_id_type=MESH,
            ).start()
        recv_n[phase, ch, me_n] = send_n[phase, ch, me_n]

    def third(phase, ch):
        rnd = phase // 2
        pltpu.make_async_copy(
            send_n.at[phase, ch, pl.ds(0, narrow - 1)],
            recv_n.at[phase, ch, pl.ds(0, narrow - 1)],
            came_n.at[phase, ch],
        ).wait()
        for p in range(PER_CHUNK // 2):
            x = jnp.concatenate(
                [
                    rows_of([
                        recv_n[phase, ch, n, pl.ds(((2 * p + q) * 2 + c) * rows_n, rows_n), :]
                        for c in range(2) for n in range(narrow)
                    ])
                    for q in range(2)
                ],
                axis=1,
            )
            y = apply(left_ref[4 * rnd + 2], x)
            for q in range(2):
                for c in range(2):
                    for w in range(wide):
                        at = ((2 * p + q) * 2 + c) * rows_w
                        send_w[phase, ch, w, at:at + rows_w, :] = y[
                            c * GATE + w * rows_w:c * GATE + (w + 1) * rows_w,
                            q * LANES:(q + 1) * LANES,
                        ]

        def push(d, _):
            to = lax.rem(me_w + d, wide)
            pltpu.make_async_remote_copy(
                src_ref=send_w.at[phase, ch, to],
                dst_ref=recv_w.at[phase, ch, me_w],
                send_sem=sent_w.at[phase, ch],
                recv_sem=came_w.at[phase, ch],
                device_id={"wide": to},
                device_id_type=MESH,
            ).start()
            return 0

        lax.fori_loop(1, wide, push, 0, unroll=wide <= 8)
        recv_w[phase, ch, me_w] = send_w[phase, ch, me_w]

    def fourth(phase, ch):
        rnd, split = phase // 2, phase % 2
        pltpu.make_async_copy(
            send_w.at[phase, ch, pl.ds(0, wide - 1)],
            recv_w.at[phase, ch, pl.ds(0, wide - 1)],
            came_w.at[phase, ch],
        ).wait()
        for p in range(PER_CHUNK // 2):
            x = jnp.concatenate(
                [
                    rows_of([
                        recv_w[phase, ch, w, pl.ds(((2 * p + q) * 2 + c) * rows_w, rows_w), :]
                        for c in range(2) for w in range(wide)
                    ])
                    for q in range(2)
                ],
                axis=1,
            )
            y = apply(left_ref[4 * rnd + 3], x)
            for q in range(2):
                unit = ch * PER_CHUNK + 2 * p + q
                start = pl.multiple_of(split * split_rows + unit * block_rows, block_rows)
                mixed[pl.ds(start, block_rows), :] = y[:, q * LANES:(q + 1) * LANES]

    def fifth(phase):
        rnd, split = phase // 2, phase % 2

        def step(i, _):
            parts = []
            for q in range(2):
                pair = [
                    rows_of([
                        mixed[pl.ds(split * split_rows + c * GATE + a * 2 + b, half, stride=block_rows), :]
                        for c in range(2) for b in range(2)
                    ])
                    for a in (2 * i + q, 2 * i + q + half)
                ]
                lower, upper = weave(*pair)
                rows = []
                for k in range(4):
                    rows += [lower[k * half:(k + 1) * half], upper[k * half:(k + 1) * half]]
                parts.append(rows_of(rows))
            y = apply(left_ref[4 * rnd + 4], jnp.concatenate(parts, axis=1))
            for q in range(2):
                ap = 2 * i + q
                mine = y[:, q * LANES:(q + 1) * LANES]
                if rnd < ROUNDS - 1 or split == 0:
                    keep(split, ap, mine)
                else:
                    for c in range(2):
                        start = pl.multiple_of(c * half * GATE + ap * GATE, GATE)
                        pair = weave(plane[pl.ds(start, GATE), :], mine[c * GATE:(c + 1) * GATE])
                        for a, part in zip((ap, ap + half), pair):
                            out_ref[pl.ds(a * block_rows + c, GATE, stride=2), :] = part
            return 0

        lax.fori_loop(0, half // 2, step, 0)

    def over_chunks(body):
        def step(ch, _):
            body(ch)
            return 0

        lax.fori_loop(0, chunks, step, 0)

    loads[2].wait()
    first(0)
    pl.semaphore_wait(barrier, narrow - 1 + wide - 1)
    over_chunks(lambda ch: second(0, ch))
    first(1)
    for rnd in range(ROUNDS):
        for i in range(max(2 - 4 * rnd, 1), 4):
            if 4 * rnd + i > 1:
                left_ref[4 * rnd + i] = left_of(bank(5 * rnd + i))
        last = bank(5 * rnd + 4)
        if rnd < ROUNDS - 1:
            last = jnp.dot(
                bank(5 * rnd + 5), last, precision=lax.Precision.HIGHEST,
                preferred_element_type=jnp.float32,
            )
        left_ref[4 * rnd + 4] = left_of(last)

    for phase in range(2 * ROUNDS):
        def exchange(ch, phase=phase):
            third(phase, ch)
            if phase + 1 < 2 * ROUNDS:
                second(phase + 1, ch)

        over_chunks(exchange)
        over_chunks(functools.partial(fourth, phase))
        fifth(phase)

    def settle(ch):
        for phase in range(2 * ROUNDS):
            pltpu.make_async_copy(
                send_n.at[phase, ch, pl.ds(0, narrow - 1)],
                recv_n.at[phase, ch, pl.ds(0, narrow - 1)],
                sent_n.at[phase, ch],
            ).wait()
            pltpu.make_async_copy(
                send_w.at[phase, ch, pl.ds(0, wide - 1)],
                recv_w.at[phase, ch, pl.ds(0, wide - 1)],
                sent_w.at[phase, ch],
            ).wait()

    over_chunks(settle)


def on_device(state, gates, roster):
    narrow, wide = lax.axis_size("narrow"), lax.axis_size("wide")
    rows = state.shape[1] // LANES
    chunks = rows // GATE // 2 // PER_CHUNK
    phases = 2 * ROUNDS
    x = state.reshape(2, rows, LANES).transpose(1, 0, 2).reshape(2 * rows, LANES)
    f32 = jnp.float32
    trade_n = pltpu.VMEM((phases, chunks, narrow, PER_CHUNK * 2 * GATE // narrow, LANES), f32)
    trade_w = pltpu.VMEM((phases, chunks, wide, PER_CHUNK * 2 * GATE // wide, LANES), f32)
    dma = pltpu.SemaphoreType.DMA((phases, chunks))
    hbm = pl.BlockSpec(memory_space=pltpu.HBM)
    whole = pltpu.VMEM((2 * rows, LANES), f32)
    out = pl.pallas_call(
        functools.partial(kernel, narrow, wide),
        out_shape=jax.ShapeDtypeStruct((2 * rows, LANES), f32),
        in_specs=[hbm, hbm, hbm],
        out_specs=pl.BlockSpec(memory_space=pltpu.VMEM),
        scratch_shapes=[
            pltpu.VMEM(gates.shape, f32),
            pltpu.SMEM(roster.shape, jnp.int32),
            whole,
            pltpu.VMEM((4 * ROUNDS + 1, 4 * GATE, 4 * GATE), jnp.bfloat16),
            whole, whole,
            trade_n, trade_n, trade_w, trade_w,
            pltpu.SemaphoreType.DMA((3,)),
            dma, dma, dma, dma,
        ],
        compiler_params=pltpu.CompilerParams(
            collective_id=0, has_side_effects=True, vmem_limit_bytes=64 * 1024 * 1024
        ),
    )(gates, roster, x)
    return out.reshape(rows, 2, LANES).transpose(1, 0, 2).reshape(2, rows * LANES)


def solution(mesh):
    in_specs = (P(None, ("wide", "narrow")), P(), P())
    out_specs = P(None, ("wide", "narrow"))
    return jax.shard_map(
        on_device, mesh=mesh, in_specs=in_specs, out_specs=out_specs, check_vma=False
    )
```

profile of v0, /device:TPU:25, one launch (start us, length us, event | category | flops | bytes accessed | tf_op | source)
XLA Modules:
  0.0 114.1 jit_solution(15337035922343872620)
XLA Ops:
  0.0 111.5 %shard_map.37 = f32[4096,128]{1,0:T(8,128)} custom-call(f32[8,2,64,64]{3,2,1,0:T(8,128)} %gates_hbm.1, s32[10]{0:T(128)} %roster_hbm.1, f32[4096,128]{1,0:T(8,128)} %bitcast.11), custom_call_target="tpu_custom_call" | custom-call | tf_op jit(solution)/shard_map/pallas_call | solution.py:314
  111.5 2.6 %copy.7 = f32[2,262144]{1,0:T(2,128)} copy(f32[2,262144]{1,0:T(2,128)} %bitcast.10) | data formatting | bytes 4194304
where the time goes:
time: 114 us
  Pallas kernels  111 us (97%)
  local copies, waits for them, and re-layouts  2.61 us (2%)
    pallas_call x1, Pallas kernels, on_device(): pl.pallas_call(functools.partial(kernel, narrow, wide), out_shape=jax.Sha...  111 us
    unnamed x1, local copies, waits for them, and re-layouts  2.61 us

commit v1 on v0

--- a/solution.py
+++ b/solution.py
@@ -10,7 +10,7 @@
 ROUNDS = 2
 GATE = 64
 LANES = 128
-PER_CHUNK = 4
+PER_CHUNK = 2
 MESH = pl.DeviceIdType.MESH
 
 
@@ -50,6 +50,19 @@
 
 def rows_of(parts):
     return jnp.concatenate(parts, axis=0)
+
+
+def farthest_first(count):
+    return [d for d in range(count // 2, count)] + [d for d in range(1, count // 2)]
+
+
+def partner(me, distance, count):
+    to, bit = 0, 1
+    while bit < count:
+        mine = lax.rem(lax.div(me, bit), 2)
+        to = to + bit * (1 - mine if distance & bit else mine)
+        bit *= 2
+    return to
 
 
 def kernel(narrow, wide, gates_hbm, roster_hbm, x_hbm, out_ref, gates_ref, roster_ref, x_ref,
@@ -136,8 +149,8 @@
                             c * GATE + n * rows_n:c * GATE + (n + 1) * rows_n,
                             q * LANES:(q + 1) * LANES,
                         ]
-        for d in range(1, narrow):
-            to = lax.rem(me_n + d, narrow)
+        for d in farthest_first(narrow):
+            to = partner(me_n, d, narrow)
             pltpu.make_async_remote_copy(
                 src_ref=send_n.at[phase, ch, to],
                 dst_ref=recv_n.at[phase, ch, me_n],
@@ -249,12 +262,12 @@
 
         lax.fori_loop(0, half // 2, step, 0)
 
-    def over_chunks(body):
+    def over_chunks(body, begin=0, end=chunks):
         def step(ch, _):
             body(ch)
             return 0
 
-        lax.fori_loop(0, chunks, step, 0)
+        lax.fori_loop(begin, end, step, 0)
 
     loads[2].wait()
     first(0)
@@ -279,8 +292,17 @@
             if phase + 1 < 2 * ROUNDS:
                 second(phase + 1, ch)
 
-        over_chunks(exchange)
-        over_chunks(functools.partial(fourth, phase))
+        if phase + 1 < 2 * ROUNDS:
+            over_chunks(exchange)
+            over_chunks(functools.partial(fourth, phase))
+        else:
+            def drain(ch, phase=phase):
+                third(phase, ch)
+                fourth(phase, ch - 2)
+
+            over_chunks(exchange, 0, 2)
+            over_chunks(drain, 2, chunks)
+            over_chunks(functools.partial(fourth, phase), chunks - 2, chunks)
         fifth(phase)
 
     def settle(ch):

time: 114 us -> 117 us (1.026)
  the two profiles are of different devices: /device:TPU:25 before, /device:TPU:9 now
where the time goes in v1:
time: 117 us; the launch traced here: 116 us
  Pallas kernels  113 us (97%)
  local copies, waits for them, and re-layouts  2.61 us (2%)
    pallas_call x1, Pallas kernels, on_device(): pl.pallas_call(functools.partial(kernel, narrow, wide), out_shape=jax.Sha...  113 us
    unnamed x1, local copies, waits for them, and re-layouts  2.61 us

profile of v1, /device:TPU:9, one launch (start us, length us, event | category | flops | bytes accessed | tf_op | source)
XLA Modules:
  0.0 115.6 jit_solution(12734529793610692852)
XLA Ops:
  0.0 113.0 %shard_map.37 = f32[4096,128]{1,0:T(8,128)} custom-call(f32[8,2,64,64]{3,2,1,0:T(8,128)} %gates_hbm.1, s32[10]{0:T(128)} %roster_hbm.1, f32[4096,128]{1,0:T(8,128)} %bitcast.11), custom_call_target="tpu_custom_call" | custom-call | tf_op jit(solution)/shard_map/pallas_call | solution.py:336
  113.0 2.6 %copy.7 = f32[2,262144]{1,0:T(2,128)} copy(f32[2,262144]{1,0:T(2,128)} %bitcast.10) | data formatting | bytes 4194304

commit v2 on v0

--- a/solution.py
+++ b/solution.py
@@ -11,6 +11,7 @@
 GATE = 64
 LANES = 128
 PER_CHUNK = 4
+PIECES = 4
 MESH = pl.DeviceIdType.MESH
 
 
@@ -52,9 +53,46 @@
     return jnp.concatenate(parts, axis=0)
 
 
-def kernel(narrow, wide, gates_hbm, roster_hbm, x_hbm, out_ref, gates_ref, roster_ref, x_ref,
-           left_ref, plane, mixed, send_n, recv_n, send_w, recv_w, load_sem,
-           sent_n, came_n, sent_w, came_w):
+def in_order(first, second):
+    lower, upper = weave(first, second)
+    half = first.shape[0] // 4
+    rows = []
+    for k in range(4):
+        rows += [lower[k * half:(k + 1) * half], upper[k * half:(k + 1) * half]]
+    return rows_of(rows)
+
+
+def closing(left_ref, kept_ref, mixed_ref, out_ref):
+    units, pairs = mixed_ref.shape[0], kept_ref.shape[1] // GATE
+    flat = mixed_ref.reshape(units * 4 * 2 * pairs, LANES)
+    left = left_ref[...]
+    for p in range(pairs // 2):
+        parts = []
+        for q in range(2):
+            ap = 2 * p + q
+            pair = [
+                rows_of([
+                    flat[pl.ds((c * 2 + h) * 2 * pairs + ap * 2 + b, units, stride=8 * pairs), :]
+                    for c in range(2) for b in range(2)
+                ])
+                for h in range(2)
+            ]
+            parts.append(in_order(*pair))
+        y = apply(left, jnp.concatenate(parts, axis=1))
+        for q in range(2):
+            ap = 2 * p + q
+            for c in range(2):
+                pair = weave(
+                    kept_ref[c, ap * GATE:(ap + 1) * GATE, :],
+                    y[c * GATE:(c + 1) * GATE, q * LANES:(q + 1) * LANES],
+                )
+                for h in range(2):
+                    out_ref[h, pl.ds(ap * 2 * GATE + c, GATE, stride=2), :] = pair[h]
+
+
+def kernel(narrow, wide, gates_hbm, roster_hbm, x_hbm, kept_hbm, mixed_hbm, last_hbm,
+           gates_ref, roster_ref, x_ref, left_ref, plane, mixed, send_n, recv_n, send_w, recv_w,
+           load_sem, x_sem, kept_sem, last_sem, mixed_sem, sent_n, came_n, sent_w, came_w):
     me_n, me_w = lax.axis_index("narrow"), lax.axis_index("wide")
     blocks = x_ref.shape[0] // (2 * GATE)
     half = blocks // 2
@@ -66,10 +104,18 @@
     loads = [
         pltpu.make_async_copy(roster_hbm, roster_ref, load_sem.at[0]),
         pltpu.make_async_copy(gates_hbm, gates_ref, load_sem.at[1]),
-        pltpu.make_async_copy(x_hbm, x_ref, load_sem.at[2]),
     ]
     for load in loads:
         load.start()
+    piece = half // PIECES
+
+    def x_load(p, h):
+        rows = pl.ds(pl.multiple_of((h * half + p * piece) * block_rows, block_rows), piece * block_rows)
+        return pltpu.make_async_copy(x_hbm.at[rows], x_ref.at[rows], x_sem.at[p, h])
+
+    for p in range(PIECES):
+        for h in range(2):
+            x_load(p, h).start()
 
     barrier = pltpu.get_barrier_semaphore()
 
@@ -111,7 +157,14 @@
                 keep(split, 2 * i + q, y[:, q * LANES:(q + 1) * LANES])
             return 0
 
-        lax.fori_loop(0, half // 2, step, 0)
+        def steps(p, _):
+            if split == 0:
+                for h in range(2):
+                    x_load(p, h).wait()
+            lax.fori_loop(p * (piece // 2), (p + 1) * (piece // 2), step, 0)
+            return 0
+
+        lax.fori_loop(0, PIECES, steps, 0)
 
     def second(phase, ch):
         rnd, split = phase // 2, phase % 2
@@ -228,23 +281,11 @@
                     ])
                     for a in (2 * i + q, 2 * i + q + half)
                 ]
-                lower, upper = weave(*pair)
-                rows = []
-                for k in range(4):
-                    rows += [lower[k * half:(k + 1) * half], upper[k * half:(k + 1) * half]]
-                parts.append(rows_of(rows))
+                parts.append(in_order(*pair))
             y = apply(left_ref[4 * rnd + 4], jnp.concatenate(parts, axis=1))
             for q in range(2):
                 ap = 2 * i + q
-                mine = y[:, q * LANES:(q + 1) * LANES]
-                if rnd < ROUNDS - 1 or split == 0:
-                    keep(split, ap, mine)
-                else:
-                    for c in range(2):
-                        start = pl.multiple_of(c * half * GATE + ap * GATE, GATE)
-                        pair = weave(plane[pl.ds(start, GATE), :], mine[c * GATE:(c + 1) * GATE])
-                        for a, part in zip((ap, ap + half), pair):
-                            out_ref[pl.ds(a * block_rows + c, GATE, stride=2), :] = part
+                keep(split, ap, y[:, q * LANES:(q + 1) * LANES])
             return 0
 
         lax.fori_loop(0, half // 2, step, 0)
@@ -256,7 +297,6 @@
 
         lax.fori_loop(0, chunks, step, 0)
 
-    loads[2].wait()
     first(0)
     pl.semaphore_wait(barrier, narrow - 1 + wide - 1)
     over_chunks(lambda ch: second(0, ch))
@@ -273,6 +313,21 @@
             )
         left_ref[4 * rnd + 4] = left_of(last)
 
+    last_out = pltpu.make_async_copy(left_ref.at[4 * ROUNDS], last_hbm, last_sem)
+    last_out.start()
+    kept_out = pltpu.make_async_copy(plane.at[pl.ds(0, split_rows)], kept_hbm, kept_sem)
+
+    def mixed_out(ch):
+        rows = PER_CHUNK * block_rows
+        start = pl.multiple_of(ch * rows, rows)
+        return pltpu.make_async_copy(
+            mixed.at[pl.ds(split_rows + start, rows)], mixed_hbm.at[pl.ds(start, rows)], mixed_sem.at[ch]
+        )
+
+    def ending(ch):
+        fourth(2 * ROUNDS - 1, ch)
+        mixed_out(ch).start()
+
     for phase in range(2 * ROUNDS):
         def exchange(ch, phase=phase):
             third(phase, ch)
@@ -280,8 +335,13 @@
                 second(phase + 1, ch)
 
         over_chunks(exchange)
-        over_chunks(functools.partial(fourth, phase))
-        fifth(phase)
+        if phase + 1 < 2 * ROUNDS:
+            over_chunks(functools.partial(fourth, phase))
+            fifth(phase)
+            if phase == 2 * ROUNDS - 2:
+                kept_out.start()
+        else:
+            over_chunks(ending)
 
     def settle(ch):
         for phase in range(2 * ROUNDS):
@@ -297,6 +357,9 @@
             ).wait()
 
     over_chunks(settle)
+    last_out.wait()
+    kept_out.wait()
+    over_chunks(lambda ch: mixed_out(ch).wait())
 
 
 def on_device(state, gates, roster):
@@ -311,11 +374,13 @@
     dma = pltpu.SemaphoreType.DMA((phases, chunks))
     hbm = pl.BlockSpec(memory_space=pltpu.HBM)
     whole = pltpu.VMEM((2 * rows, LANES), f32)
-    out = pl.pallas_call(
+    half_state = jax.ShapeDtypeStruct((rows, LANES), f32)
+    factor = jax.ShapeDtypeStruct((4 * GATE, 4 * GATE), jnp.bfloat16)
+    kept, mixed, last = pl.pallas_call(
         functools.partial(kernel, narrow, wide),
-        out_shape=jax.ShapeDtypeStruct((2 * rows, LANES), f32),
+        out_shape=[half_state, half_state, factor],
         in_specs=[hbm, hbm, hbm],
-        out_specs=pl.BlockSpec(memory_space=pltpu.VMEM),
+        out_specs=[hbm, hbm, hbm],
         scratch_shapes=[
             pltpu.VMEM(gates.shape, f32),
             pltpu.SMEM(roster.shape, jnp.int32),
@@ -323,13 +388,31 @@
             pltpu.VMEM((4 * ROUNDS + 1, 4 * GATE, 4 * GATE), jnp.bfloat16),
             whole, whole,
             trade_n, trade_n, trade_w, trade_w,
-            pltpu.SemaphoreType.DMA((3,)),
+            pltpu.SemaphoreType.DMA((2,)),
+            pltpu.SemaphoreType.DMA((PIECES, 2)),
+            pltpu.SemaphoreType.DMA, pltpu.SemaphoreType.DMA,
+            pltpu.SemaphoreType.DMA((chunks,)),
             dma, dma, dma, dma,
         ],
         compiler_params=pltpu.CompilerParams(
             collective_id=0, has_side_effects=True, vmem_limit_bytes=64 * 1024 * 1024
         ),
     )(gates, roster, x)
+
+    half = rows // GATE // 2
+    pairs = half // PIECES
+    out = pl.pallas_call(
+        closing,
+        grid=(PIECES,),
+        out_shape=jax.ShapeDtypeStruct((2, rows, LANES), f32),
+        in_specs=[
+            pl.BlockSpec((4 * GATE, 4 * GATE), lambda i: (0, 0)),
+            pl.BlockSpec((2, pairs * GATE, LANES), lambda i: (0, i, 0)),
+            pl.BlockSpec((half, 2, 2, 2 * pairs, LANES), lambda i: (0, 0, 0, i, 0)),
+        ],
+        out_specs=pl.BlockSpec((2, pairs * 2 * GATE, LANES), lambda i: (0, i, 0)),
+        compiler_params=pltpu.CompilerParams(vmem_limit_bytes=64 * 1024 * 1024),
+    )(last, kept.reshape(2, half * GATE, LANES), mixed.reshape(half, 2, 2, GATE // 2, LANES))
     return out.reshape(rows, 2, LANES).transpose(1, 0, 2).reshape(2, rows * LANES)
 
 

time: 114 us -> 113 us (level)
  the two profiles are of different devices: /device:TPU:25 before, /device:TPU:27 now
where the time goes in v2:
time: 113 us
  Pallas kernels  113 us (100%)
    pallas_call x1, Pallas kernels, on_device(): pl.pallas_call(functools.partial(kernel, narrow, wide), out_shape=[half_s...  108 us
    pallas_call x1, Pallas kernels, on_device(): pl.pallas_call(closing, grid=(PIECES,), out_shape=jax.ShapeDtypeStruct((2...  4.84 us

profile of v2, /device:TPU:27, one launch (start us, length us, event | category | flops | bytes accessed | tf_op | source)
XLA Modules:
  0.0 112.6 jit_solution(2616538498745798063)
XLA Ops:
  0.0 107.8 %shard_map.37 = (f32[2048,128]{1,0:T(8,128)}, f32[2048,128]{1,0:T(8,128)}, bf16[256,256]{1,0:T(8,128)(2,1)}) custom-call(f32[8,2,64,64]{3,2,1,0:T(8,128)} %gates_hbm.1, s32[10]{0:T(128)} %roster_hbm.1, f32[4096,128]{1,0:T(8,128)} %bitcast.12), custom_call_target="tpu_custom_call" | custom-call | tf_op jit(solution)/shard_map/pallas_call | solution.py:379
  107.8 4.8 %shard_map.38 = f32[2,2048,128]{2,1,0:T(8,128)} custom-call(bf16[256,256]{1,0:T(8,128)(2,1)} %get-tuple-element.8.left_ref, f32[2,1024,128]{2,1,0:T(8,128)} %bitcast.13, f32[16,2,2,32,128]{4,3,2,1,0:T(8,128)} %bitcast.14), custom_call_target="tpu_custom_call" | custom-call | tf_op jit(solution)/shard_map/pallas_call | solution.py:404

commit v3 on v2

--- a/solution.py
+++ b/solution.py
@@ -12,6 +12,7 @@
 LANES = 128
 PER_CHUNK = 4
 PIECES = 4
+AT_ONCE = 4
 MESH = pl.DeviceIdType.MESH
 
 
@@ -66,10 +67,10 @@
     units, pairs = mixed_ref.shape[0], kept_ref.shape[1] // GATE
     flat = mixed_ref.reshape(units * 4 * 2 * pairs, LANES)
     left = left_ref[...]
-    for p in range(pairs // 2):
+    for p in range(pairs // AT_ONCE):
         parts = []
-        for q in range(2):
-            ap = 2 * p + q
+        for q in range(AT_ONCE):
+            ap = AT_ONCE * p + q
             pair = [
                 rows_of([
                     flat[pl.ds((c * 2 + h) * 2 * pairs + ap * 2 + b, units, stride=8 * pairs), :]
@@ -79,8 +80,8 @@
             ]
             parts.append(in_order(*pair))
         y = apply(left, jnp.concatenate(parts, axis=1))
-        for q in range(2):
-            ap = 2 * p + q
+        for q in range(AT_ONCE):
+            ap = AT_ONCE * p + q
             for c in range(2):
                 pair = weave(
                     kept_ref[c, ap * GATE:(ap + 1) * GATE, :],
@@ -88,6 +89,19 @@
                 )
                 for h in range(2):
                     out_ref[h, pl.ds(ap * 2 * GATE + c, GATE, stride=2), :] = pair[h]
+
+
+def farthest_first(count):
+    return [d for d in range(count // 2, count)] + [d for d in range(1, count // 2)]
+
+
+def partner(me, distance, count):
+    to, bit = 0, 1
+    while bit < count:
+        mine = lax.rem(lax.div(me, bit), 2)
+        to = to + bit * (1 - mine if distance & bit else mine)
+        bit *= 2
+    return to
 
 
 def kernel(narrow, wide, gates_hbm, roster_hbm, x_hbm, kept_hbm, mixed_hbm, last_hbm,
@@ -146,51 +160,50 @@
     def first(split):
         def step(i, _):
             parts = []
-            for q in range(2):
+            for q in range(AT_ONCE):
                 pair = [
                     rows_of([x_ref[pl.ds(a * block_rows + c, GATE, stride=2), :] for c in range(2)])
-                    for a in (2 * i + q, 2 * i + q + half)
+                    for a in (AT_ONCE * i + q, AT_ONCE * i + q + half)
                 ]
                 parts.append(weave(*pair)[split])
             y = apply(left_ref[0], jnp.concatenate(parts, axis=1))
-            for q in range(2):
-                keep(split, 2 * i + q, y[:, q * LANES:(q + 1) * LANES])
+            for q in range(AT_ONCE):
+                keep(split, AT_ONCE * i + q, y[:, q * LANES:(q + 1) * LANES])
             return 0
 
         def steps(p, _):
             if split == 0:
                 for h in range(2):
                     x_load(p, h).wait()
-            lax.fori_loop(p * (piece // 2), (p + 1) * (piece // 2), step, 0)
+            lax.fori_loop(p * (piece // AT_ONCE), (p + 1) * (piece // AT_ONCE), step, 0)
             return 0
 
         lax.fori_loop(0, PIECES, steps, 0)
 
     def second(phase, ch):
         rnd, split = phase // 2, phase % 2
-        for p in range(PER_CHUNK // 2):
-            parts = []
-            for q in range(2):
-                unit = ch * PER_CHUNK + 2 * p + q
-                rows = []
-                for c in range(2):
-                    base = split * split_rows + c * half * GATE + unit
-                    rows += weave(
-                        plane[pl.ds(base, blocks, stride=blocks), :],
-                        plane[pl.ds(base + half, blocks, stride=blocks), :],
-                    )
-                parts.append(rows_of(rows))
-            y = apply(left_ref[4 * rnd + 1], jnp.concatenate(parts, axis=1))
-            for q in range(2):
-                for c in range(2):
-                    for n in range(narrow):
-                        at = ((2 * p + q) * 2 + c) * rows_n
-                        send_n[phase, ch, n, at:at + rows_n, :] = y[
-                            c * GATE + n * rows_n:c * GATE + (n + 1) * rows_n,
-                            q * LANES:(q + 1) * LANES,
-                        ]
-        for d in range(1, narrow):
-            to = lax.rem(me_n + d, narrow)
+        parts = []
+        for q in range(PER_CHUNK):
+            unit = ch * PER_CHUNK + q
+            rows = []
+            for c in range(2):
+                base = split * split_rows + c * half * GATE + unit
+                rows += weave(
+                    plane[pl.ds(base, blocks, stride=blocks), :],
+                    plane[pl.ds(base + half, blocks, stride=blocks), :],
+                )
+            parts.append(rows_of(rows))
+        y = apply(left_ref[4 * rnd + 1], jnp.concatenate(parts, axis=1))
+        for q in range(PER_CHUNK):
+            for c in range(2):
+                for n in range(narrow):
+                    at = (q * 2 + c) * rows_n
+                    send_n[phase, ch, n, at:at + rows_n, :] = y[
+                        c * GATE + n * rows_n:c * GATE + (n + 1) * rows_n,
+                        q * LANES:(q + 1) * LANES,
+                    ]
+        for d in farthest_first(narrow):
+            to = partner(me_n, d, narrow)
             pltpu.make_async_remote_copy(
                 src_ref=send_n.at[phase, ch, to],
                 dst_ref=recv_n.at[phase, ch, me_n],
@@ -208,26 +221,25 @@
             recv_n.at[phase, ch, pl.ds(0, narrow - 1)],
             came_n.at[phase, ch],
         ).wait()
-        for p in range(PER_CHUNK // 2):
-            x = jnp.concatenate(
-                [
-                    rows_of([
-                        recv_n[phase, ch, n, pl.ds(((2 * p + q) * 2 + c) * rows_n, rows_n), :]
-                        for c in range(2) for n in range(narrow)
-                    ])
-                    for q in range(2)
-                ],
-                axis=1,
-            )
-            y = apply(left_ref[4 * rnd + 2], x)
-            for q in range(2):
-                for c in range(2):
-                    for w in range(wide):
-                        at = ((2 * p + q) * 2 + c) * rows_w
-                        send_w[phase, ch, w, at:at + rows_w, :] = y[
-                            c * GATE + w * rows_w:c * GATE + (w + 1) * rows_w,
-                            q * LANES:(q + 1) * LANES,
-                        ]
+        x = jnp.concatenate(
+            [
+                rows_of([
+                    recv_n[phase, ch, n, pl.ds((q * 2 + c) * rows_n, rows_n), :]
+                    for c in range(2) for n in range(narrow)
+                ])
+                for q in range(PER_CHUNK)
+            ],
+            axis=1,
+        )
+        y = apply(left_ref[4 * rnd + 2], x)
+        for q in range(PER_CHUNK):
+            for c in range(2):
+                for w in range(wide):
+                    at = (q * 2 + c) * rows_w
+                    send_w[phase, ch, w, at:at + rows_w, :] = y[
+                        c * GATE + w * rows_w:c * GATE + (w + 1) * rows_w,
+                        q * LANES:(q + 1) * LANES,
+                    ]
 
         def push(d, _):
             to = lax.rem(me_w + d, wide)
@@ -251,44 +263,43 @@
             recv_w.at[phase, ch, pl.ds(0, wide - 1)],
             came_w.at[phase, ch],
         ).wait()
-        for p in range(PER_CHUNK // 2):
-            x = jnp.concatenate(
-                [
-                    rows_of([
-                        recv_w[phase, ch, w, pl.ds(((2 * p + q) * 2 + c) * rows_w, rows_w), :]
-                        for c in range(2) for w in range(wide)
-                    ])
-                    for q in range(2)
-                ],
-                axis=1,
-            )
-            y = apply(left_ref[4 * rnd + 3], x)
-            for q in range(2):
-                unit = ch * PER_CHUNK + 2 * p + q
-                start = pl.multiple_of(split * split_rows + unit * block_rows, block_rows)
-                mixed[pl.ds(start, block_rows), :] = y[:, q * LANES:(q + 1) * LANES]
+        x = jnp.concatenate(
+            [
+                rows_of([
+                    recv_w[phase, ch, w, pl.ds((q * 2 + c) * rows_w, rows_w), :]
+                    for c in range(2) for w in range(wide)
+                ])
+                for q in range(PER_CHUNK)
+            ],
+            axis=1,
+        )
+        y = apply(left_ref[4 * rnd + 3], x)
+        for q in range(PER_CHUNK):
+            unit = ch * PER_CHUNK + q
+            start = pl.multiple_of(split * split_rows + unit * block_rows, block_rows)
+            mixed[pl.ds(start, block_rows), :] = y[:, q * LANES:(q + 1) * LANES]
 
     def fifth(phase):
         rnd, split = phase // 2, phase % 2
 
         def step(i, _):
             parts = []
-            for q in range(2):
+            for q in range(AT_ONCE):
                 pair = [
                     rows_of([
                         mixed[pl.ds(split * split_rows + c * GATE + a * 2 + b, half, stride=block_rows), :]
                         for c in range(2) for b in range(2)
                     ])
-                    for a in (2 * i + q, 2 * i + q + half)
+                    for a in (AT_ONCE * i + q, AT_ONCE * i + q + half)
                 ]
                 parts.append(in_order(*pair))
             y = apply(left_ref[4 * rnd + 4], jnp.concatenate(parts, axis=1))
-            for q in range(2):
-                ap = 2 * i + q
+            for q in range(AT_ONCE):
+                ap = AT_ONCE * i + q
                 keep(split, ap, y[:, q * LANES:(q + 1) * LANES])
             return 0
 
-        lax.fori_loop(0, half // 2, step, 0)
+        lax.fori_loop(0, half // AT_ONCE, step, 0)
 
     def over_chunks(body):
         def step(ch, _):

time: 113 us -> 113 us (level)
  the two profiles are of different devices: /device:TPU:27 before, /device:TPU:9 now
where the time goes in v3:
time: 113 us
  Pallas kernels  113 us (100%)
    pallas_call x1, Pallas kernels, on_device(): pl.pallas_call(functools.partial(kernel, narrow, wide), out_shape=[half_s...  108 us
    pallas_call x1, Pallas kernels, on_device(): pl.pallas_call(closing, grid=(PIECES,), out_shape=jax.ShapeDtypeStruct((2...  4.84 us

profile of v3, /device:TPU:9, one launch (start us, length us, event | category | flops | bytes accessed | tf_op | source)
XLA Modules:
  0.0 112.6 jit_solution(1806277355148473911)
XLA Ops:
  0.0 107.7 %shard_map.37 = (f32[2048,128]{1,0:T(8,128)}, f32[2048,128]{1,0:T(8,128)}, bf16[256,256]{1,0:T(8,128)(2,1)}) custom-call(f32[8,2,64,64]{3,2,1,0:T(8,128)} %gates_hbm.1, s32[10]{0:T(128)} %roster_hbm.1, f32[4096,128]{1,0:T(8,128)} %bitcast.12), custom_call_target="tpu_custom_call" | custom-call | tf_op jit(solution)/shard_map/pallas_call | solution.py:390
  107.7 4.8 %shard_map.38 = f32[2,2048,128]{2,1,0:T(8,128)} custom-call(bf16[256,256]{1,0:T(8,128)(2,1)} %get-tuple-element.8.left_ref, f32[2,1024,128]{2,1,0:T(8,128)} %bitcast.13, f32[16,2,2,32,128]{4,3,2,1,0:T(8,128)} %bitcast.14), custom_call_target="tpu_custom_call" | custom-call | tf_op jit(solution)/shard_map/pallas_call | solution.py:415

commit v4 on v3

--- a/solution.py
+++ b/solution.py
@@ -13,6 +13,7 @@
 PER_CHUNK = 4
 PIECES = 4
 AT_ONCE = 4
+STEPS = 2
 MESH = pl.DeviceIdType.MESH
 
 
@@ -91,19 +92,6 @@
                     out_ref[h, pl.ds(ap * 2 * GATE + c, GATE, stride=2), :] = pair[h]
 
 
-def farthest_first(count):
-    return [d for d in range(count // 2, count)] + [d for d in range(1, count // 2)]
-
-
-def partner(me, distance, count):
-    to, bit = 0, 1
-    while bit < count:
-        mine = lax.rem(lax.div(me, bit), 2)
-        to = to + bit * (1 - mine if distance & bit else mine)
-        bit *= 2
-    return to
-
-
 def kernel(narrow, wide, gates_hbm, roster_hbm, x_hbm, kept_hbm, mixed_hbm, last_hbm,
            gates_ref, roster_ref, x_ref, left_ref, plane, mixed, send_n, recv_n, send_w, recv_w,
            load_sem, x_sem, kept_sem, last_sem, mixed_sem, sent_n, came_n, sent_w, came_w):
@@ -202,8 +190,8 @@
                         c * GATE + n * rows_n:c * GATE + (n + 1) * rows_n,
                         q * LANES:(q + 1) * LANES,
                     ]
-        for d in farthest_first(narrow):
-            to = partner(me_n, d, narrow)
+        for d in range(1, narrow):
+            to = lax.rem(me_n + lax.rem(me_w, 2) * (narrow - 2 * d) + d, narrow)
             pltpu.make_async_remote_copy(
                 src_ref=send_n.at[phase, ch, to],
                 dst_ref=recv_n.at[phase, ch, me_n],
@@ -411,10 +399,10 @@
     )(gates, roster, x)
 
     half = rows // GATE // 2
-    pairs = half // PIECES
+    pairs = half // STEPS
     out = pl.pallas_call(
         closing,
-        grid=(PIECES,),
+        grid=(STEPS,),
         out_shape=jax.ShapeDtypeStruct((2, rows, LANES), f32),
         in_specs=[
             pl.BlockSpec((4 * GATE, 4 * GATE), lambda i: (0, 0)),

time: 113 us -> 112 us (level)
  no operation moved by 1% of the time
where the time goes in v4:
time: 112 us
  Pallas kernels  112 us (100%)
    pallas_call x1, Pallas kernels, on_device(): pl.pallas_call(functools.partial(kernel, narrow, wide), out_shape=[half_s...  108 us
    pallas_call x1, Pallas kernels, on_device(): pl.pallas_call(closing, grid=(STEPS,), out_shape=jax.ShapeDtypeStruct((2,...  3.76 us

profile of v4, /device:TPU:9, one launch (start us, length us, event | category | flops | bytes accessed | tf_op | source)
XLA Modules:
  0.0 111.6 jit_solution(10292847841229446443)
XLA Ops:
  0.0 107.8 %shard_map.37 = (f32[2048,128]{1,0:T(8,128)}, f32[2048,128]{1,0:T(8,128)}, bf16[256,256]{1,0:T(8,128)(2,1)}) custom-call(f32[8,2,64,64]{3,2,1,0:T(8,128)} %gates_hbm.1, s32[10]{0:T(128)} %roster_hbm.1, f32[4096,128]{1,0:T(8,128)} %bitcast.12), custom_call_target="tpu_custom_call" | custom-call | tf_op jit(solution)/shard_map/pallas_call | solution.py:378
  107.8 3.8 %shard_map.38 = f32[2,2048,128]{2,1,0:T(8,128)} custom-call(bf16[256,256]{1,0:T(8,128)(2,1)} %get-tuple-element.8.left_ref, f32[2,1024,128]{2,1,0:T(8,128)} %bitcast.13, f32[16,2,2,32,128]{4,3,2,1,0:T(8,128)} %bitcast.14), custom_call_target="tpu_custom_call" | custom-call | tf_op jit(solution)/shard_map/pallas_call | solution.py:403

commit v5 on v4

--- a/solution.py
+++ b/solution.py
@@ -190,8 +190,9 @@
                         c * GATE + n * rows_n:c * GATE + (n + 1) * rows_n,
                         q * LANES:(q + 1) * LANES,
                     ]
+        back = lax.rem(me_w, 2) * lax.rem(ch, 2)
         for d in range(1, narrow):
-            to = lax.rem(me_n + lax.rem(me_w, 2) * (narrow - 2 * d) + d, narrow)
+            to = lax.rem(me_n + back * (narrow - 2 * d) + d, narrow)
             pltpu.make_async_remote_copy(
                 src_ref=send_n.at[phase, ch, to],
                 dst_ref=recv_n.at[phase, ch, me_n],
@@ -327,23 +328,8 @@
         fourth(2 * ROUNDS - 1, ch)
         mixed_out(ch).start()
 
-    for phase in range(2 * ROUNDS):
-        def exchange(ch, phase=phase):
-            third(phase, ch)
-            if phase + 1 < 2 * ROUNDS:
-                second(phase + 1, ch)
-
-        over_chunks(exchange)
-        if phase + 1 < 2 * ROUNDS:
-            over_chunks(functools.partial(fourth, phase))
-            fifth(phase)
-            if phase == 2 * ROUNDS - 2:
-                kept_out.start()
-        else:
-            over_chunks(ending)
-
-    def settle(ch):
-        for phase in range(2 * ROUNDS):
+    def settle(phases, ch):
+        for phase in phases:
             pltpu.make_async_copy(
                 send_n.at[phase, ch, pl.ds(0, narrow - 1)],
                 recv_n.at[phase, ch, pl.ds(0, narrow - 1)],
@@ -355,7 +341,23 @@
                 sent_w.at[phase, ch],
             ).wait()
 
-    over_chunks(settle)
+    for phase in range(2 * ROUNDS):
+        def exchange(ch, phase=phase):
+            third(phase, ch)
+            if phase + 1 < 2 * ROUNDS:
+                second(phase + 1, ch)
+
+        over_chunks(exchange)
+        if phase + 1 < 2 * ROUNDS:
+            over_chunks(functools.partial(fourth, phase))
+            fifth(phase)
+            if phase == 2 * ROUNDS - 2:
+                kept_out.start()
+                over_chunks(functools.partial(settle, range(2 * ROUNDS - 1)))
+        else:
+            over_chunks(ending)
+
+    over_chunks(functools.partial(settle, [2 * ROUNDS - 1]))
     last_out.wait()
     kept_out.wait()
     over_chunks(lambda ch: mixed_out(ch).wait())

time: 112 us -> 110 us (0.982)
  Pallas kernels: 112 us -> 109 us
    pallas_call x1, Pallas kernels: 108 us -> 106 us  [on_device(): pl.pallas_call(functools.partial(kernel, narrow, wide), out_shape=[half_s...]
where the time goes in v5:
time: 110 us; the launch traced here: 109 us
  Pallas kernels  109 us (99%)
    pallas_call x1, Pallas kernels, on_device(): pl.pallas_call(functools.partial(kernel, narrow, wide), out_shape=[half_s...  106 us
    pallas_call x1, Pallas kernels, on_device(): pl.pallas_call(closing, grid=(STEPS,), out_shape=jax.ShapeDtypeStruct((2,...  3.76 us

profile of v5, /device:TPU:9, one launch (start us, length us, event | category | flops | bytes accessed | tf_op | source)
XLA Modules:
  0.0 109.3 jit_solution(4561295781772429692)
XLA Ops:
  0.0 105.6 %shard_map.37 = (f32[2048,128]{1,0:T(8,128)}, f32[2048,128]{1,0:T(8,128)}, bf16[256,256]{1,0:T(8,128)(2,1)}) custom-call(f32[8,2,64,64]{3,2,1,0:T(8,128)} %gates_hbm.1, s32[10]{0:T(128)} %roster_hbm.1, f32[4096,128]{1,0:T(8,128)} %bitcast.12), custom_call_target="tpu_custom_call" | custom-call | tf_op jit(solution)/shard_map/pallas_call | solution.py:380
  105.6 3.8 %shard_map.38 = f32[2,2048,128]{2,1,0:T(8,128)} custom-call(bf16[256,256]{1,0:T(8,128)(2,1)} %get-tuple-element.8.left_ref, f32[2,1024,128]{2,1,0:T(8,128)} %bitcast.13, f32[16,2,2,32,128]{4,3,2,1,0:T(8,128)} %bitcast.14), custom_call_target="tpu_custom_call" | custom-call | tf_op jit(solution)/shard_map/pallas_call | solution.py:405

commit v6 on v5

--- a/solution.py
+++ b/solution.py
@@ -231,7 +231,7 @@
                     ]
 
         def push(d, _):
-            to = lax.rem(me_w + d, wide)
+            to = lax.rem(me_w + lax.rem(me_w, 2) * (wide - 2 * d) + d, wide)
             pltpu.make_async_remote_copy(
                 src_ref=send_w.at[phase, ch, to],
                 dst_ref=recv_w.at[phase, ch, me_w],

time: 110 us -> 110 us (level)
  no operation moved by 1% of the time
where the time goes in v6:
time: 110 us; the launch traced here: 109 us
  Pallas kernels  109 us (99%)
    pallas_call x1, Pallas kernels, on_device(): pl.pallas_call(functools.partial(kernel, narrow, wide), out_shape=[half_s...  106 us
    pallas_call x1, Pallas kernels, on_device(): pl.pallas_call(closing, grid=(STEPS,), out_shape=jax.ShapeDtypeStruct((2,...  3.76 us

profile of v6, /device:TPU:9, one launch (start us, length us, event | category | flops | bytes accessed | tf_op | source)
XLA Modules:
  0.0 109.3 jit_solution(14071467335517516762)
XLA Ops:
  0.0 105.6 %shard_map.37 = (f32[2048,128]{1,0:T(8,128)}, f32[2048,128]{1,0:T(8,128)}, bf16[256,256]{1,0:T(8,128)(2,1)}) custom-call(f32[8,2,64,64]{3,2,1,0:T(8,128)} %gates_hbm.1, s32[10]{0:T(128)} %roster_hbm.1, f32[4096,128]{1,0:T(8,128)} %bitcast.12), custom_call_target="tpu_custom_call" | custom-call | tf_op jit(solution)/shard_map/pallas_call | solution.py:380
  105.6 3.8 %shard_map.38 = f32[2,2048,128]{2,1,0:T(8,128)} custom-call(bf16[256,256]{1,0:T(8,128)(2,1)} %get-tuple-element.8.left_ref, f32[2,1024,128]{2,1,0:T(8,128)} %bitcast.13, f32[16,2,2,32,128]{4,3,2,1,0:T(8,128)} %bitcast.14), custom_call_target="tpu_custom_call" | custom-call | tf_op jit(solution)/shard_map/pallas_call | solution.py:405
